TPU v7x, 512 devices: a whole 4x4x16 slice. The times are simulated.
512 devices in a mesh: dp: 64 (over z_hi, x, y), tensor: 8 (over z_lo, core).
Axes of the slice: x: 4, y: 4, z: 16 (z_hi: 4, z_lo: 4; z = z_hi * 4 + z_lo), core: 2. Of those that a mesh axis runs over, the one named last changes fastest.
Arguments:
- activations: bfloat16 [32768, 8192], P('dp', 'tensor'), may hold values from -6 to 6
- projection_basis: bfloat16 [8192, 512], P('tensor'), may hold values from -0.0625 to 0.0625
- cotangent: bfloat16 [64, 8, 28, 32768], P(None, 'tensor', None, 'dp'), may hold values from -0.09375 to 0.09375
- first_moment: float32 [64, 8, 28, 512], P('dp', 'tensor'), may hold values from -3 to 3
- second_moment: float32 [64, 8, 28, 512], P('dp', 'tensor'), may hold values from 0.05 to 2
Outputs:
- new_first: float32 [64, 8, 28, 512], P('dp', 'tensor')
- new_second: float32 [64, 8, 28, 512], P('dp', 'tensor')
- weight_update: bfloat16 [8192, 64, 224], P('tensor', 'dp')
All inputs are finite; a program needn't handle non-finite values.
Results may differ from a plain program's by a relative error of at most 0.005.
Values may be sent and summed in bfloat16 or wider, within the bound.
A program may use at most 64 MiB of HBM per device.

v0:
```python
import jax
import jax.numpy as jnp
from jax import lax
from jax.sharding import PartitionSpec as P

STEP = 100


def per_device(activations, projection_basis, cotangent, first_moment, second_moment):
    partial_proj = jnp.dot(activations, projection_basis, preferred_element_type=jnp.float32)
    projected = lax.psum(partial_proj, "tensor").astype(jnp.bfloat16)
    block_count = cotangent.shape[0]
    col_count = cotangent.shape[2]
    token_count = cotangent.shape[3]
    cotangent_rows = cotangent.reshape(block_count * col_count, token_count)
    partial_terms = jnp.dot(cotangent_rows, projected, preferred_element_type=jnp.float32)
    low_rank_grad = lax.psum_scatter(partial_terms, "dp", scatter_dimension=0, tiled=True)
    low_rank_grad = low_rank_grad.reshape(first_moment.shape)
    new_first = 0.9 * first_moment + 0.1 * low_rank_grad
    new_second = 0.999 * second_moment + 0.001 * low_rank_grad * low_rank_grad
    first_scale = 1.0 - 0.9**STEP
    second_scale = 1.0 - 0.999**STEP
    direction = new_first / first_scale / (jnp.sqrt(new_second / second_scale) + 1e-08)
    direction = direction.astype(jnp.bfloat16).reshape(col_count, direction.shape[3])
    update_local = lax.dot_general(
        projection_basis,
        lax.all_gather(direction, "tensor", axis=0, tiled=True),
        (((1,), (1,)), ((), ())),
        preferred_element_type=jnp.float32,
    )
    weight_update = update_local.astype(jnp.bfloat16).reshape(
        projection_basis.shape[0], 1, update_local.shape[1]
    )
    return (new_first, new_second, weight_update)


def solution(mesh):
    in_specs = (
        P("dp", "tensor"),
        P("tensor", None),
        P(None, "tensor", None, "dp"),
        P("dp", "tensor", None, None),
        P("dp", "tensor", None, None),
    )
    out_specs = (
        P("dp", "tensor", None, None),
        P("dp", "tensor", None, None),
        P("tensor", "dp", None),
    )
    return jax.shard_map(
        per_device, mesh=mesh, in_specs=in_specs, out_specs=out_specs, check_vma=False
    )
```

profile of v0, /device:TPU:1, one launch (start us, length us, event | category | flops | bytes accessed | tf_op | source)
XLA Modules:
  0.0 977.2 jit_solution(11178600964761212466)
XLA Ops:
  7.2 0.0 copy-start
  7.2 0.0 all-reduce.4.cloned.1.call-start
  7.2 2.6 copy.24
  9.8 1.5 reshape.19
  11.3 0.0 copy-done
  11.3 0.0 copy-start.1
  11.3 3.1 fusion.7
  14.3 62.5 %all-reduce.5 = bf16[512,512]{1,0:T(8,128)(2,1)S(1)} all-reduce(f32[512,512]{1,0:T(8,128)} %fusion.7), channel_id=1, replica_groups=mesh['dp'=64,'tensor'=8] {'tensor'}, use_global_device_ids=true, to_apply=%region_0.0 | all-reduce | flops 262144 | bytes 1572864 | tf_op jit(solution)/shard_map/psum | solution.py:11
  76.9 0.0 copy-done.1
  76.9 3.0 convolution_bitcast_fusion
  79.9 0.0 copy-start.2
  79.9 0.0 copy-start.3
  79.9 0.0 all-reduce.4.cloned.1.call-update
  79.9 0.8 copy-done.2
  80.7 0.1 copy.23
  80.9 0.0 copy-done.3
  80.9 0.1 copy.25
  81.0 1.3 dynamic-slice
  82.9 825.6 %all-reduce.4.cloned.1.call-done = f32[1792,512]{0,1:T(8,128)} async-done(((f32[1792,512]{0,1:T(8,128)}), f32[1792,512]{0,1:T(8,128)}) %all-reduce.4.cloned.1.call-update) | async-done | bytes 3670032
  908.5 1.3 divide_convert_fusion
  909.8 0.2 copy.26
  910.0 57.6 %all-gather = bf16[1,1,224,512]{3,1,0,2:T(2,128)(2,1)S(1)} all-gather(bf16[1,1,28,512]{3,1,0,2:T(2,128)(2,1)S(1)} %copy.26), channel_id=2, replica_groups=mesh['dp'=64,'tensor'=8] {'tensor'}, dimensions={2}, use_global_device_ids=true | all-gather | bytes 258048 | tf_op jit(solution)/shard_map/all_gather | solution.py:27
  967.6 1.3 fusion
  968.8 0.7 copy.27
  969.6 0.7 copy.28
Async XLA Ops:
  7.2 4.1 copy-start
  7.2 901.3 %all-reduce.4.cloned.1.call-start = ((), (), s32[]{:S(2)}) async-start(), calls=%async_computation | async-start | bytes 7340032
  11.3 65.6 %copy-start.1 = (bf16[1792,512]{1,0:T(8,128)(2,1)S(1)}, bf16[1792,512]{1,0:T(8,128)(2,1)}, u32[]{:S(2)}) copy-start(bf16[1792,512]{1,0:T(8,128)(2,1)} %reshape.19) | copy-start | bytes 5505028
  79.9 0.8 copy-start.2
  79.9 1.0 copy-start.3
Sparse Core Ops, SparseCore 0:
  80.0 828.4 all-reduce.3
where the time goes:
time: 978 us; the launch traced here: 977 us
  waiting for transfers between devices  826 us (84%)
  blocking collectives  120 us (12%)
  between operations  14.8 us (2%)
    unnamed x2, waiting for transfers between devices  826 us
    psum x1, blocking collectives, per_device(): projected = lax.psum(partial_proj, 'tensor').astype(jnp.bfloat16)  62.5 us
    all_gather x1, blocking collectives, per_device(): lax.all_gather(direction, 'tensor', axis=0, tiled=True)  57.6 us
  transfers between devices with their start and end apart: 1, of which 1 were waited for; matrix products, arithmetic and copies ran while one was open for 0% of the time, Pallas kernels for 0%

commit v1 on v0

v1 whole, which is shorter than its diff:
```python
import functools

import jax
import jax.numpy as jnp
from jax import lax
from jax.experimental import pallas as pl
from jax.experimental.pallas import tpu as pltpu
from jax.sharding import PartitionSpec as P

STEP = 100
CH = 4
KC = 128
SLOTS = 21
MESH = pl.DeviceIdType.MESH
F32, BF16 = jnp.float32, jnp.bfloat16

X0, E, M, T, TC, XY1, XY2, ZH, AG, AGC = 0, 1, 2, 3, 4, 5, 8, 11, 14, 17


def kernel(
    act_hbm, basis_hbm, cot_hbm, m1_hbm, m2_hbm,
    nf_ref, ns_ref, wu_ref,
    act, basis, cot, cotf, cperm, m1, m2, nfs, nss,
    x0s, x0r, acc, sb, er, mb, mr, proj,
    p2, r1, g, r2, hs, zs, r3, dirs, wide, lhs,
    in_sem, send_sem, recv_sem,
):
    dp, tensor = lax.axis_index("dp"), lax.axis_index("tensor")
    zh, x, y = dp // 16, (dp // 4) % 4, dp % 4
    zl, c = tensor // 2, tensor % 2
    mid = jnp.logical_or(zl == 1, zl == 2)
    end = jnp.logical_not(mid)

    def at(zh=zh, x=x, y=y, zl=zl, c=c):
        return (zh * 16 + x * 4 + y, zl * 2 + c)

    def turn(v, i):
        return (v + i) % 4

    other_core = at(c=1 - c)
    pair = at(zl=zl + 1 - 2 * (zl % 2))
    middle = at(zl=3 - zl)
    xs = [at(x=turn(x, i)) for i in (1, 2, 3)]
    ys = [at(y=turn(y, i)) for i in (1, 2, 3)]
    zhs = [at(zh=turn(zh, i)) for i in (1, 2, 3)]
    zls = [at(zl=turn(zl, i)) for i in (1, 2, 3)]

    barrier = pltpu.get_barrier_semaphore()
    for device in [other_core] + zls + xs + ys + zhs:
        pl.semaphore_signal(barrier, inc=1, device_id=device, device_id_type=MESH)

    loads = [
        pltpu.make_async_copy(act_hbm, act, in_sem.at[0]),
        pltpu.make_async_copy(basis_hbm, basis, in_sem.at[1]),
        pltpu.make_async_copy(cot_hbm, cot, in_sem.at[2]),
        pltpu.make_async_copy(m1_hbm, m1.at[pl.ds(0, 112)], in_sem.at[3]),
        pltpu.make_async_copy(m2_hbm, m2.at[pl.ds(0, 112)], in_sem.at[4]),
    ]
    for load in loads:
        load.start()

    def copy(k, slot, src, dst, device):
        i = k * SLOTS + slot
        return pltpu.make_async_remote_copy(
            src, dst, send_sem.at[i], recv_sem.at[i], device_id=device, device_id_type=MESH
        )

    mine = pl.ds(pl.multiple_of(c * 256, 256), 256)
    theirs = pl.ds(pl.multiple_of((1 - c) * 256, 256), 256)

    def cp_x0(k):
        return copy(k, X0, x0s.at[k], x0r.at[k], other_core)

    def cp_e(k):
        return copy(k, E, sb.at[k], er.at[k], pair)

    def cp_m(k):
        return copy(k, M, mb.at[k], mr.at[k], middle)

    def cp_t(k):
        return copy(k, T, proj.at[k, mine], proj.at[k, mine], pair)

    def cp_tc(k):
        return copy(k, TC, proj.at[k, mine], proj.at[k, mine], other_core)

    def tc_arrival(k):
        return copy(k, TC, proj.at[k, theirs], proj.at[k, theirs], other_core)

    def cp_1(k, i):
        if k % 2 == 0:
            return copy(k, XY1 + i, p2.at[k, turn(x, i + 1)], r1.at[k, i], xs[i])
        return copy(k, XY1 + i, p2.at[k, :, turn(y, i + 1)], r1.at[k, i], ys[i])

    def cp_2(k, i):
        if k % 2 == 0:
            return copy(k, XY2 + i, g.at[k, turn(y, i + 1)], r2.at[k, i], ys[i])
        return copy(k, XY2 + i, g.at[k, turn(x, i + 1)], r2.at[k, i], xs[i])

    def cp_z(k, i):
        return copy(k, ZH + i, zs.at[k, turn(zh, i + 1)], r3.at[k, i], zhs[i])

    def cp_ag(k, i):
        return copy(k, AG + i, dirs.at[k, tensor], dirs.at[k, tensor], zls[i])

    def ag_arrival(k, i):
        slot = dirs.at[k, turn(zl, 3 - i) * 2 + c]
        return copy(k, AG + i, slot, slot, zls[i])

    def cp_agc(k, i):
        slot = dirs.at[k, turn(zl, 4 - i) * 2 + c]
        return copy(k, AGC + i, slot, slot, other_core)

    def agc_arrival(k, i):
        slot = dirs.at[k, turn(zl, 4 - i) * 2 + 1 - c]
        return copy(k, AGC + i, slot, slot, other_core)

    for buf in (hs,):
        for k in range(CH):
            buf[k, pl.ds(112, 16)] = jnp.zeros((16, KC), F32)
    m1[pl.ds(112, 16)] = jnp.zeros((16, KC), F32)
    m2[pl.ds(112, 16)] = jnp.zeros((16, KC), F32)
    loads[0].wait()
    loads[1].wait()
    out = jnp.dot(act[theirs, :], basis[...], preferred_element_type=F32)
    for k in range(CH):
        x0s[k] = out[:, k * KC : (k + 1) * KC].astype(BF16)
    out = jnp.dot(act[mine, :], basis[...], preferred_element_type=F32)
    for k in range(CH):
        acc[k] = out[:, k * KC : (k + 1) * KC]
    loads[2].wait()
    for n in range(4):
        cotf[n] = cot[:, n * 128 : (n + 1) * 128].astype(F32)
    for n in range(4):
        for b in range(16):
            cperm[pl.ds(b * 112, 112), n * 128 : (n + 1) * 128] = cotf[n, pl.ds(b, 112, stride=16), :].astype(BF16)
    pl.semaphore_wait(barrier, 13)

    def s0(k):
        cp_x0(k).start()

    def s1(k):
        cp_x0(k).wait_recv()
        total = acc[k] + x0r[k].astype(F32)
        acc[k] = total

        @pl.when(end)
        def _():
            sb[k] = total.astype(BF16)
            cp_e(k).start()

    def s2(k):
        @pl.when(mid)
        def _():
            cp_e(k).wait_recv()
            total = acc[k] + er[k].astype(F32)
            acc[k] = total
            mb[k] = total.astype(BF16)
            cp_m(k).start()

    def s3(k):
        @pl.when(mid)
        def _():
            cp_m(k).wait_recv()
            proj[k, mine] = (acc[k] + mr[k].astype(F32)).astype(BF16)
            cp_t(k).start()

        @pl.when(end)
        def _():
            cp_t(k).wait_recv()

        cp_tc(k).start()

    def s4(k):
        tc_arrival(k).wait_recv()
        out = jnp.dot(cperm[...], proj[k], preferred_element_type=F32)
        p2[k] = out.astype(BF16).reshape(4, 4, 112, KC)
        for i in range(3):
            cp_1(k, i).start()

    def s5(k):
        own = p2[k, x] if k % 2 == 0 else p2[k, :, y]
        total = own.astype(F32)
        for i in range(3):
            cp_1(k, i).wait_recv()
            total = total + r1[k, i].astype(F32)
        g[k] = total.astype(BF16)
        for i in range(3):
            cp_2(k, i).start()

    def s6(k):
        own = g[k, y] if k % 2 == 0 else g[k, x]
        total = own.astype(F32)
        for i in range(3):
            cp_2(k, i).wait_recv()
            total = total + r2[k, i].astype(F32)
        hs[k, pl.ds(0, 112)] = total
        for z in range(4):
            zs[k, z] = hs[k, pl.ds(z, 32, stride=4), :].astype(BF16)
        for i in range(3):
            cp_z(k, i).start()

    def s7(k):
        grad = zs[k, zh].astype(F32)
        for i in range(3):
            cp_z(k, i).wait_recv()
            grad = grad + r3[k, i].astype(F32)
        rows = pl.ds(k, 32, stride=4)
        new_first = 0.9 * m1[rows, :] + 0.1 * grad
        new_second = 0.999 * m2[rows, :] + 0.001 * grad * grad
        nfs[rows, :] = new_first
        nss[rows, :] = new_second
        direction = new_first / (1.0 - 0.9**STEP) / (jnp.sqrt(new_second / (1.0 - 0.999**STEP)) + 1e-08)
        dirs[k, tensor] = direction.astype(BF16)
        for i in range(3):
            cp_ag(k, i).start()
        cp_agc(k, 0).start()

    def s8(k):
        for i in range(3):
            ag_arrival(k, i).wait_recv()
            cp_agc(k, i + 1).start()

    def s9(k):
        for i in range(4):
            agc_arrival(k, i).wait_recv()
        for t in range(8):
            wide[k, pl.ds(t * 28, 32)] = dirs[k, t].astype(F32)
        lhs[:, k * KC : (k + 1) * KC] = wide[k, pl.ds(0, 224)].astype(BF16)

    for stage in (s0, s1, s2, s3, s4, s5, s6):
        for k in range(CH):
            stage(k)
    loads[3].wait()
    loads[4].wait()
    for stage in (s7, s8, s9):
        for k in range(CH):
            stage(k)
    nf_ref[...] = nfs[pl.ds(0, 112)]
    ns_ref[...] = nss[pl.ds(0, 112)]
    wu_ref[...] = lax.dot_general(
        lhs[...], basis[...], (((1,), (1,)), ((), ())), preferred_element_type=F32
    ).astype(BF16)

    for k in range(CH):
        cp_x0(k).wait_send()
        cp_tc(k).wait_send()
        for i in range(3):
            cp_1(k, i).wait_send()
            cp_2(k, i).wait_send()
            cp_z(k, i).wait_send()
            cp_ag(k, i).wait_send()
        for i in range(4):
            cp_agc(k, i).wait_send()

    @pl.when(end)
    def _():
        for k in range(CH):
            cp_e(k).wait_send()

    @pl.when(mid)
    def _():
        for k in range(CH):
            cp_m(k).wait_send()
            cp_t(k).wait_send()


def per_device(activations, projection_basis, cotangent, first_moment, second_moment):
    cot = jnp.transpose(cotangent, (1, 2, 0, 3)).reshape(1792, 512)
    vmem = functools.partial(pltpu.VMEM)
    nf, ns, wu = pl.pallas_call(
        kernel,
        out_shape=(
            jax.ShapeDtypeStruct((112, 128), F32),
            jax.ShapeDtypeStruct((112, 128), F32),
            jax.ShapeDtypeStruct((224, 1024), BF16),
        ),
        in_specs=[pl.BlockSpec(memory_space=pl.ANY)] * 5,
        out_specs=[pl.BlockSpec(memory_space=pltpu.VMEM)] * 3,
        scratch_shapes=[
            vmem((512, 1024), BF16),
            vmem((1024, 512), BF16),
            vmem((1792, 512), BF16),
            vmem((4, 1792, 128), F32),
            vmem((1792, 512), BF16),
            vmem((128, 128), F32),
            vmem((128, 128), F32),
            vmem((128, 128), F32),
            vmem((128, 128), F32),
            vmem((CH, 256, KC), BF16),
            vmem((CH, 256, KC), BF16),
            vmem((CH, 256, KC), F32),
            vmem((CH, 256, KC), BF16),
            vmem((CH, 256, KC), BF16),
            vmem((CH, 256, KC), BF16),
            vmem((CH, 256, KC), BF16),
            vmem((CH, 512, KC), BF16),
            vmem((CH, 4, 4, 112, KC), BF16),
            vmem((CH, 3, 4, 112, KC), BF16),
            vmem((CH, 4, 112, KC), BF16),
            vmem((CH, 3, 112, KC), BF16),
            vmem((CH, 128, KC), F32),
            vmem((CH, 4, 32, KC), BF16),
            vmem((CH, 3, 32, KC), BF16),
            vmem((CH, 8, 32, KC), BF16),
            vmem((CH, 232, KC), F32),
            vmem((224, 512), BF16),
            pltpu.SemaphoreType.DMA((5,)),
            pltpu.SemaphoreType.DMA((CH * SLOTS,)),
            pltpu.SemaphoreType.DMA((CH * SLOTS,)),
        ],
        compiler_params=pltpu.CompilerParams(
            collective_id=0, has_side_effects=True, vmem_limit_bytes=63 << 20
        ),
        name="galore_step",
    )(
        activations,
        projection_basis,
        cot,
        first_moment.reshape(112, 128),
        second_moment.reshape(112, 128),
    )
    return (
        nf.reshape(first_moment.shape),
        ns.reshape(second_moment.shape),
        jnp.transpose(wu).reshape(1024, 1, 224),
    )


def solution(mesh):
    in_specs = (
        P("dp", "tensor"),
        P("tensor", None),
        P(None, "tensor", None, "dp"),
        P("dp", "tensor", None, None),
        P("dp", "tensor", None, None),
    )
    out_specs = (
        P("dp", "tensor", None, None),
        P("dp", "tensor", None, None),
        P("tensor", "dp", None),
    )
    return jax.shard_map(
        per_device, mesh=mesh, in_specs=in_specs, out_specs=out_specs, check_vma=False
    )
```

time: 978 us -> 72.9 us (0.07)
  waiting for transfers between devices: 826 us -> 0 us
  blocking collectives: 120 us -> 0 us
  Pallas kernels: 0 us -> 67.3 us
  between operations: 14.8 us -> 0.64 us
    unnamed x2 -> x0, waiting for transfers between devices: 826 us -> none
    pallas_call x0 -> x1, Pallas kernels: none -> 67.3 us  [per_device(): pl.pallas_call(kernel, out_shape=(jax.ShapeDtypeStruct((112, 128), F32),...]
    psum x1 -> x0, blocking collectives: 62.5 us -> none  [per_device(): projected = lax.psum(partial_proj, 'tensor').astype(jnp.bfloat16)]
    all_gather x1 -> x0, blocking collectives: 57.6 us -> none  [per_device(): lax.all_gather(direction, 'tensor', axis=0, tiled=True)]
  transfers between devices with their start and end apart: 1 -> 0, of which waited for: 1 -> 0; matrix products, arithmetic and copies ran while one was open for 0% -> 0% of each run, Pallas kernels for 0% -> 0%
where the time goes in v1:
time: 72.9 us; the launch traced here: 72.6 us
  Pallas kernels  67.3 us (92%)
  local copies, waits for them, and re-layouts  4.7 us (6%)
    pallas_call x1, Pallas kernels, per_device(): pl.pallas_call(kernel, out_shape=(jax.ShapeDtypeStruct((112, 128), F32),...  67.3 us
    unnamed x3, local copies, waits for them, and re-layouts  4.7 us

profile of v1, /device:TPU:1, one launch (start us, length us, event | category | flops | bytes accessed | tf_op | source)
XLA Modules:
  0.0 72.6 jit_solution(4416592551375204295)
XLA Ops:
  0.6 67.3 %galore_step.1 = (f32[112,128]{1,0:T(8,128)}, f32[112,128]{1,0:T(8,128)}, bf16[224,1024]{1,0:T(8,128)(2,1)}) custom-call(bf16[512,1024]{1,0:T(8,128)(2,1)} %act_hbm.1, bf16[1024,512]{1,0:T(8,128)(2,1)} %basis_hbm.1, bf16[1792,512]{1,0:T(8,128)(2,1)} %bitcast.10, f32[112,128]{1,0:T(8,128)} %bitcast.12, f32[112,128]{1,0:T(8,128)} %bitcast.13), custom_call_target="tpu_custom_call" | custom-call | tf_op jit(solution)/shard_map/galore_step/pallas_call | solution.py:270
  67.9 1.4 %copy.15 = f32[1,1,28,512]{3,1,2,0:T(1,128)} copy(f32[1,1,28,512]{3,1,2,0:T(1,128)} %bitcast.15) | data formatting | bytes 114688
  69.4 1.4 %copy.16 = f32[1,1,28,512]{3,1,2,0:T(1,128)} copy(f32[1,1,28,512]{3,1,2,0:T(1,128)} %bitcast.14) | data formatting | bytes 114688
  70.8 1.8 %copy.17 = bf16[1024,1,224]{0,2,1:T(8,128)(2,1)} copy(bf16[1024,1,224]{0,2,1:T(8,128)(2,1)} %bitcast.11) | data formatting | bytes 917504

commit v2 on v0

v2 whole, which is shorter than its diff:
```python
import functools

import jax
import jax.numpy as jnp
from jax import lax
from jax.experimental import pallas as pl
from jax.experimental.pallas import tpu as pltpu
from jax.sharding import PartitionSpec as P

STEP = 100
CH = 4
KC = 128
MESH = pl.DeviceIdType.MESH
F32, BF16 = jnp.float32, jnp.bfloat16

X0 = 0
E = X0 + CH
M = E + 2 * CH
T = M + 2 * CH
TC = T + 2 * CH
XY1 = TC + CH
XY2 = XY1 + 6 * CH
ZH = XY2 + 3 * CH
AG = ZH + 3 * CH // 2
SEMS = AG + 7 * CH // 2


def kernel(
    act_hbm, basis_hbm, cot_hbm, m1_hbm, m2_hbm,
    grad_ref, lhs_ref,
    act, basis, cot, cotf, cperm, m1, m2,
    x0s, x0r, acc, sb, er, mb, mr, proj,
    p2, ra, rb, rc, g, r2, hs, zs, r3, dirs, wide, grads,
    in_sem, send_sem, recv_sem,
):
    dp, tensor = lax.axis_index("dp"), lax.axis_index("tensor")
    zh, x, y = dp // 16, (dp // 4) % 4, dp % 4
    zl, c = tensor // 2, tensor % 2
    mid = jnp.logical_or(zl == 1, zl == 2)
    end = jnp.logical_not(mid)

    def at(zh=zh, x=x, y=y, zl=zl, c=c):
        return (zh * 16 + x * 4 + y, zl * 2 + c)

    def turn(v, i):
        return (v + i) % 4

    other_core = at(c=1 - c)
    pair = at(zl=zl + 1 - 2 * (zl % 2))
    middle = at(zl=3 - zl)
    xs = [at(x=turn(x, i)) for i in (1, 2, 3)]
    ys = [at(y=turn(y, i)) for i in (1, 2, 3)]
    zhs = [at(zh=turn(zh, i)) for i in (1, 2, 3)]
    steps = [(i, e) for i in range(4) for e in range(2)][1:]
    tensors = [at(zl=turn(zl, i), c=(c + e) % 2) for i, e in steps]

    barrier = pltpu.get_barrier_semaphore()
    for device in zhs + tensors + xs + ys:
        pl.semaphore_signal(barrier, inc=1, device_id=device, device_id_type=MESH)

    mine = pl.ds(pl.multiple_of(c * 256, 256), 256)
    theirs = pl.ds(pl.multiple_of((1 - c) * 256, 256), 256)

    loads = [
        pltpu.make_async_copy(basis_hbm, basis, in_sem.at[0]),
        pltpu.make_async_copy(act_hbm.at[theirs], act.at[theirs], in_sem.at[1]),
        pltpu.make_async_copy(act_hbm.at[mine], act.at[mine], in_sem.at[2]),
        pltpu.make_async_copy(cot_hbm, cot, in_sem.at[3]),
        pltpu.make_async_copy(m1_hbm, m1.at[pl.ds(0, 112)], in_sem.at[4]),
        pltpu.make_async_copy(m2_hbm, m2.at[pl.ds(0, 112)], in_sem.at[5]),
    ]
    for load in loads[:3]:
        load.start()

    def copy(i, src, dst, device):
        return pltpu.make_async_remote_copy(
            src, dst, send_sem.at[i], recv_sem.at[i], device_id=device, device_id_type=MESH
        )

    def half(h):
        return pl.ds(h * 128, 128)

    def proj_half(k, h):
        return proj.at[k, pl.ds(pl.multiple_of(c * 256 + h * 128, 128), 128)]

    def cp_x0(k):
        return copy(X0 + k, x0s.at[k], x0r.at[k], other_core)

    def cp_e(k, h):
        return copy(E + 2 * k + h, sb.at[k, half(h)], er.at[k, half(h)], pair)

    def cp_m(k, h):
        return copy(M + 2 * k + h, mb.at[k, half(h)], mr.at[k, half(h)], middle)

    def cp_t(k, h):
        return copy(T + 2 * k + h, proj_half(k, h), proj_half(k, h), pair)

    def cp_tc(k):
        return copy(TC + k, proj.at[k, mine], proj.at[k, mine], other_core)

    def tc_arrival(k):
        return copy(TC + k, proj.at[k, theirs], proj.at[k, theirs], other_core)

    def part(k, i, h):
        if k % 2 == 0:
            return p2.at[k, turn(x, i), pl.ds(2 * h, 2)]
        return p2.at[k, pl.ds(2 * h, 2), turn(y, i)]

    def cp_1(k, n):
        ring = xs if k % 2 == 0 else ys
        plus, minus = ring[0], ring[2]
        src, dst, device = (
            (part(k, 2, 0), ra.at[k, 0], plus),
            (part(k, 2, 1), ra.at[k, 1], minus),
            (part(k, 1, 1), rb.at[k, 0], plus),
            (part(k, 3, 0), rb.at[k, 1], minus),
            (part(k, 1, 0), rc.at[k, 0], plus),
            (part(k, 3, 1), rc.at[k, 1], minus),
        )[n]
        return copy(XY1 + 6 * k + n, src, dst, device)

    def cp_2(k, i):
        v, ring = (y, ys) if k % 2 == 0 else (x, xs)
        return copy(XY2 + 3 * k + i, g.at[k, turn(v, i + 1)], r2.at[k, i], ring[i])

    def cp_z(p, i):
        return copy(ZH + 3 * p + i, zs.at[p, turn(zh, i + 1)], r3.at[p, i], zhs[i])

    def cp_ag(p, n):
        return copy(AG + 7 * p + n, dirs.at[p, tensor], dirs.at[p, tensor], tensors[n])

    def ag_arrival(p, n):
        i, e = steps[n]
        slot = dirs.at[p, turn(zl, 4 - i) * 2 + (c + e) % 2]
        return copy(AG + 7 * p + n, slot, slot, tensors[n])

    loads[0].wait()
    loads[1].wait()
    for load in loads[3:]:
        load.start()
    out = jnp.dot(act[theirs, :], basis[...], preferred_element_type=F32)
    for k in range(CH):
        x0s[k] = out[:, k * KC : (k + 1) * KC].astype(BF16)
    pl.semaphore_wait(barrier, 16)
    for k in range(CH):
        cp_x0(k).start()
    loads[2].wait()
    out = jnp.dot(act[mine, :], basis[...], preferred_element_type=F32)
    for k in range(CH):
        acc[k] = out[:, k * KC : (k + 1) * KC]

    for k in range(CH):
        cp_x0(k).wait_recv()
        total = acc[k] + x0r[k].astype(F32)
        acc[k] = total

        @pl.when(end)
        def _():
            for h in range(2):
                sb[k, half(h)] = total[h * 128 : (h + 1) * 128].astype(BF16)
                cp_e(k, h).start()

    loads[3].wait()
    for n in range(4):
        cotf[n] = cot[:, n * 128 : (n + 1) * 128].astype(F32)
    for n in range(4):
        for b in range(16):
            cperm[pl.ds(b * 112, 112), n * 128 : (n + 1) * 128] = cotf[n, pl.ds(b, 112, stride=16), :].astype(BF16)
    for k in range(CH):
        hs[k, pl.ds(112, 16)] = jnp.zeros((16, KC), F32)
    m1[pl.ds(112, 16)] = jnp.zeros((16, KC), F32)
    m2[pl.ds(112, 16)] = jnp.zeros((16, KC), F32)

    def from_end(i):
        k, h = i // 2, i % 2
        cp_e(k, h).wait_recv()
        total = acc[k, half(h)] + er[k, half(h)].astype(F32)
        acc[k, half(h)] = total
        mb[k, half(h)] = total.astype(BF16)
        cp_m(k, h).start()

    def from_middle(i):
        k, h = i // 2, i % 2
        cp_m(k, h).wait_recv()
        rows = pl.ds(pl.multiple_of(c * 256 + h * 128, 128), 128)
        proj[k, rows] = (acc[k, half(h)] + mr[k, half(h)].astype(F32)).astype(BF16)
        cp_t(k, h).start()
        if h == 1:
            cp_tc(k).start()

    def to_end(i):
        k, h = i // 2, i % 2
        cp_t(k, h).wait_recv()
        if h == 1:
            cp_tc(k).start()

    def multiply(k):
        tc_arrival(k).wait_recv()
        out = jnp.dot(cperm[...], proj[k], preferred_element_type=F32)
        p2[k] = out.astype(BF16).reshape(4, 4, 112, KC)
        for n in range(4):
            cp_1(k, n).start()

    def pass_on(k):
        for h in range(2):
            cp_1(k, h).wait_recv()
            ref = part(k, 1 + 2 * h, h)
            ref[...] = (ref[...].astype(F32) + ra[k, h].astype(F32)).astype(BF16)
            cp_1(k, 4 + h).start()

    def first_sum(k):
        for h in range(2):
            cp_1(k, 3 - h).wait_recv()
            cp_1(k, 4 + h).wait_recv()
            total = part(k, 0, h)[...].astype(F32) + rb[k, 1 - h].astype(F32) + rc[k, h].astype(F32)
            g[k, pl.ds(2 * h, 2)] = total.astype(BF16)
        for i in range(3):
            cp_2(k, i).start()

    def second_sum(k):
        total = g[k, y if k % 2 == 0 else x].astype(F32)
        for i in range(3):
            cp_2(k, i).wait_recv()
            total = total + r2[k, i].astype(F32)
        hs[k, pl.ds(0, 112)] = total
        for z in range(4):
            zs[k // 2, z, k % 2] = hs[k, pl.ds(z, 32, stride=4), :].astype(BF16)
        if k % 2 == 1:
            for i in range(3):
                cp_z(k // 2, i).start()

    def adam(p):
        grad = zs[p, zh].astype(F32)
        for i in range(3):
            cp_z(p, i).wait_recv()
            grad = grad + r3[p, i].astype(F32)
        for j in range(2):
            rows = pl.ds(2 * p + j, 32, stride=4)
            low_rank = grad[j]
            grads[rows, :] = low_rank
            new_first = 0.9 * m1[rows, :] + 0.1 * low_rank
            new_second = 0.999 * m2[rows, :] + 0.001 * low_rank * low_rank
            direction = new_first / (1.0 - 0.9**STEP) / (jnp.sqrt(new_second / (1.0 - 0.999**STEP)) + 1e-08)
            dirs[p, tensor, j] = direction.astype(BF16)
        for n in range(7):
            cp_ag(p, n).start()

    def gathered(p):
        for n in range(7):
            ag_arrival(p, n).wait_recv()
        for j in range(2):
            k = 2 * p + j
            for t in range(8):
                wide[k, pl.ds(t * 28, 32)] = dirs[p, t, j].astype(F32)
            lhs_ref[:, k * KC : (k + 1) * KC] = wide[k, pl.ds(0, 224)].astype(BF16)

    @pl.when(mid)
    def _():
        for i in range(5):
            from_end(i)
        for i in range(3):
            from_middle(i)
            from_end(5 + i)
        from_middle(3)

    @pl.when(end)
    def _():
        for i in range(4):
            to_end(i)

    multiply(0)

    @pl.when(mid)
    def _():
        for i in (4, 5, 6):
            from_middle(i)

    @pl.when(end)
    def _():
        for i in (4, 5):
            to_end(i)

    multiply(1)

    @pl.when(mid)
    def _():
        from_middle(7)

    @pl.when(end)
    def _():
        for i in (6, 7):
            to_end(i)

    multiply(2)
    pass_on(0)
    multiply(3)
    for k in range(1, CH):
        pass_on(k)
    for k in range(CH):
        first_sum(k)
    for k in range(CH):
        second_sum(k)
    loads[4].wait()
    loads[5].wait()
    adam(0)
    adam(1)
    grad_ref[...] = grads[pl.ds(0, 112)]
    gathered(0)
    gathered(1)

    for k in range(CH):
        cp_x0(k).wait_send()
        cp_tc(k).wait_send()
        for n in range(6):
            cp_1(k, n).wait_send()
        for i in range(3):
            cp_2(k, i).wait_send()
    for p in range(CH // 2):
        for i in range(3):
            cp_z(p, i).wait_send()
        for n in range(7):
            cp_ag(p, n).wait_send()

    @pl.when(end)
    def _():
        for k in range(CH):
            for h in range(2):
                cp_e(k, h).wait_send()

    @pl.when(mid)
    def _():
        for k in range(CH):
            for h in range(2):
                cp_m(k, h).wait_send()
                cp_t(k, h).wait_send()


def per_device(activations, projection_basis, cotangent, first_moment, second_moment):
    cot = jnp.transpose(cotangent, (1, 2, 0, 3)).reshape(1792, 512)
    first, second = first_moment.reshape(112, 128), second_moment.reshape(112, 128)
    vmem = functools.partial(pltpu.VMEM)
    low_rank_grad, directions = pl.pallas_call(
        kernel,
        out_shape=(
            jax.ShapeDtypeStruct((112, 128), F32),
            jax.ShapeDtypeStruct((224, 512), BF16),
        ),
        in_specs=[pl.BlockSpec(memory_space=pltpu.HBM)] * 5,
        out_specs=[pl.BlockSpec(memory_space=pltpu.VMEM)] * 2,
        scratch_shapes=[
            vmem((512, 1024), BF16),
            vmem((1024, 512), BF16),
            vmem((1792, 512), BF16),
            vmem((4, 1792, 128), F32),
            vmem((1792, 512), BF16),
            vmem((128, 128), F32),
            vmem((128, 128), F32),
            vmem((CH, 256, KC), BF16),
            vmem((CH, 256, KC), BF16),
            vmem((CH, 256, KC), F32),
            vmem((CH, 256, KC), BF16),
            vmem((CH, 256, KC), BF16),
            vmem((CH, 256, KC), BF16),
            vmem((CH, 256, KC), BF16),
            vmem((CH, 512, KC), BF16),
            vmem((CH, 4, 4, 112, KC), BF16),
            vmem((CH, 2, 2, 112, KC), BF16),
            vmem((CH, 2, 2, 112, KC), BF16),
            vmem((CH, 2, 2, 112, KC), BF16),
            vmem((CH, 4, 112, KC), BF16),
            vmem((CH, 3, 112, KC), BF16),
            vmem((CH, 128, KC), F32),
            vmem((CH // 2, 4, 2, 32, KC), BF16),
            vmem((CH // 2, 3, 2, 32, KC), BF16),
            vmem((CH // 2, 8, 2, 32, KC), BF16),
            vmem((CH, 232, KC), F32),
            vmem((128, 128), F32),
            pltpu.SemaphoreType.DMA((6,)),
            pltpu.SemaphoreType.DMA((SEMS,)),
            pltpu.SemaphoreType.DMA((SEMS,)),
        ],
        compiler_params=pltpu.CompilerParams(
            collective_id=0, has_side_effects=True, vmem_limit_bytes=213 << 18
        ),
        name="galore_step",
    )(activations, projection_basis, cot, first, second)
    new_first = 0.9 * first + 0.1 * low_rank_grad
    new_second = 0.999 * second + 0.001 * low_rank_grad * low_rank_grad
    update = lax.dot_general(
        directions, projection_basis, (((1,), (1,)), ((), ())), preferred_element_type=F32
    ).astype(BF16)
    return (
        new_first.reshape(first_moment.shape),
        new_second.reshape(second_moment.shape),
        jnp.transpose(update).reshape(1024, 1, 224),
    )


def solution(mesh):
    in_specs = (
        P("dp", "tensor"),
        P("tensor", None),
        P(None, "tensor", None, "dp"),
        P("dp", "tensor", None, None),
        P("dp", "tensor", None, None),
    )
    out_specs = (
        P("dp", "tensor", None, None),
        P("dp", "tensor", None, None),
        P("tensor", "dp", None),
    )
    return jax.shard_map(
        per_device, mesh=mesh, in_specs=in_specs, out_specs=out_specs, check_vma=False
    )
```

time: 978 us -> 62.9 us (0.06)
  waiting for transfers between devices: 826 us -> 0 us
  blocking collectives: 120 us -> 0 us
  Pallas kernels: 0 us -> 58.5 us
  between operations: 14.8 us -> 0.65 us
    unnamed x2 -> x0, waiting for transfers between devices: 826 us -> none
    psum x1 -> x0, blocking collectives: 62.5 us -> none  [per_device(): projected = lax.psum(partial_proj, 'tensor').astype(jnp.bfloat16)]
    pallas_call x0 -> x1, Pallas kernels: none -> 58.5 us  [per_device(): pl.pallas_call(kernel, out_shape=(jax.ShapeDtypeStruct((112, 128), F32),...]
    all_gather x1 -> x0, blocking collectives: 57.6 us -> none  [per_device(): lax.all_gather(direction, 'tensor', axis=0, tiled=True)]
  transfers between devices with their start and end apart: 1 -> 0, of which waited for: 1 -> 0; matrix products, arithmetic and copies ran while one was open for 0% -> 0% of each run, Pallas kernels for 0% -> 0%
where the time goes in v2:
time: 62.9 us; the launch traced here: 62.7 us
  Pallas kernels  58.5 us (93%)
  local copies, waits for them, and re-layouts  1.63 us (3%)
  matrix products  1.26 us (2%)
  other arithmetic  0.66 us (1%)
  between operations  0.65 us (1%)
    pallas_call x1, Pallas kernels, per_device(): pl.pallas_call(kernel, out_shape=(jax.ShapeDtypeStruct((112, 128), F32),...  58.5 us
    unnamed x6, local copies, waits for them, and re-layouts  1.63 us

profile of v2, /device:TPU:1, one launch (start us, length us, event | category | flops | bytes accessed | tf_op | source)
XLA Modules:
  0.0 62.7 jit_solution(5537924335383567175)
XLA Ops:
  0.6 0.0 copy-start
  0.6 0.8 %copy-done = f32[1,1,28,512]{3,1,2,0:T(1,128)S(1)} copy-done((f32[1,1,28,512]{3,1,2,0:T(1,128)S(1)}, f32[1,1,28,512]{3,1,2,0:T(1,128)}, u32[]{:S(2)}) %copy-start) | copy-done | bytes 57368
  1.5 0.0 copy-start.1
  1.5 0.8 %copy-done.1 = f32[1,1,28,512]{3,1,2,0:T(1,128)S(1)} copy-done((f32[1,1,28,512]{3,1,2,0:T(1,128)S(1)}, f32[1,1,28,512]{3,1,2,0:T(1,128)}, u32[]{:S(2)}) %copy-start.1) | copy-done | bytes 57368
  2.3 0.0 copy-start.2
  2.3 58.5 %galore_step.1 = (f32[112,128]{1,0:T(8,128)S(1)}, bf16[224,512]{1,0:T(8,128)(2,1)S(1)}) custom-call(bf16[512,1024]{1,0:T(8,128)(2,1)} %act_hbm.1, bf16[1024,512]{1,0:T(8,128)(2,1)} %basis_hbm.1, bf16[1792,512]{1,0:T(8,128)(2,1)} %bitcast.17, f32[112,128]{1,0:T(8,128)S(1)} %bitcast.13, f32[112,128]{1,0:T(8,128)S(1)} %bitcast.15), custom_call_target="tpu_custom_call" | custom-call | tf_op jit(solution)/shard_map/galore_step/pallas_call | solution.py:342
  60.7 0.7 %fusion.1 = (f32[112,128]{1,0:T(8,128)}, f32[112,128]{1,0:T(8,128)}) fusion(f32[112,128]{1,0:T(8,128)S(1)} %get-tuple-element.5, f32[112,128]{1,0:T(8,128)S(1)} %bitcast.16, f32[112,128]{1,0:T(8,128)S(1)} %bitcast.14), kind=kLoop, calls=%fused_computation.3 | loop fusion | flops 100352 | bytes 286720 | tf_op jit(solution)/shard_map/add | solution.py:388
  61.4 0.0 copy-done.2
  61.4 1.3 %fusion = bf16[1024,1,224]{0,2,1:T(8,128)(2,1)} fusion(bf16[224,512]{1,0:T(8,128)(2,1)S(1)} %get-tuple-element.6, bf16[1024,512]{1,0:T(8,128)(2,1)S(1)} %copy-done.2), kind=kOutput, calls=%fused_computation.1 | convolution fusion | flops 235110400 | bytes 1736704 | tf_op jit(solution)/shard_map/dot_general | solution.py:389
Async XLA Ops:
  0.6 0.8 %copy-start = (f32[1,1,28,512]{3,1,2,0:T(1,128)S(1)}, f32[1,1,28,512]{3,1,2,0:T(1,128)}, u32[]{:S(2)}) copy-start(f32[1,1,28,512]{3,1,2,0:T(1,128)} %param.8) | copy-start | bytes 172036
  1.5 0.8 %copy-start.1 = (f32[1,1,28,512]{3,1,2,0:T(1,128)S(1)}, f32[1,1,28,512]{3,1,2,0:T(1,128)}, u32[]{:S(2)}) copy-start(f32[1,1,28,512]{3,1,2,0:T(1,128)} %param.9) | copy-start | bytes 172036
  2.3 59.1 %copy-start.2 = (bf16[1024,512]{1,0:T(8,128)(2,1)S(1)}, bf16[1024,512]{1,0:T(8,128)(2,1)}, u32[]{:S(2)}) copy-start(bf16[1024,512]{1,0:T(8,128)(2,1)} %basis_hbm.1) | copy-start | bytes 3145732

commit v3 on v2

--- a/solution.py
+++ b/solution.py
@@ -333,6 +333,29 @@
             for h in range(2):
                 cp_m(k, h).wait_send()
                 cp_t(k, h).wait_send()
+
+
+def finish(grad_ref, lhs_ref, basis_ref, m1_ref, m2_ref, nf_hbm, ns_hbm, wu_hbm, nf, ns, wu, sem):
+    outs = [
+        pltpu.make_async_copy(nf, nf_hbm, sem.at[0]),
+        pltpu.make_async_copy(ns, ns_hbm, sem.at[1]),
+    ] + [
+        pltpu.make_async_copy(wu.at[:, pl.ds(n * 512, 512)], wu_hbm.at[:, pl.ds(n * 512, 512)], sem.at[2 + n])
+        for n in range(2)
+    ]
+    low_rank = grad_ref[...]
+    nf[...] = 0.9 * m1_ref[...] + 0.1 * low_rank
+    ns[...] = 0.999 * m2_ref[...] + 0.001 * low_rank * low_rank
+    outs[0].start()
+    outs[1].start()
+    for n in range(2):
+        wu[:, n * 512 : (n + 1) * 512] = lax.dot_general(
+            lhs_ref[...], basis_ref[n * 512 : (n + 1) * 512, :], (((1,), (1,)), ((), ())),
+            preferred_element_type=F32,
+        ).astype(BF16)
+        outs[2 + n].start()
+    for out in outs:
+        out.wait()
 
 
 def per_device(activations, projection_basis, cotangent, first_moment, second_moment):
@@ -384,11 +407,24 @@
         ),
         name="galore_step",
     )(activations, projection_basis, cot, first, second)
-    new_first = 0.9 * first + 0.1 * low_rank_grad
-    new_second = 0.999 * second + 0.001 * low_rank_grad * low_rank_grad
-    update = lax.dot_general(
-        directions, projection_basis, (((1,), (1,)), ((), ())), preferred_element_type=F32
-    ).astype(BF16)
+    new_first, new_second, update = pl.pallas_call(
+        finish,
+        out_shape=(
+            jax.ShapeDtypeStruct((112, 128), F32),
+            jax.ShapeDtypeStruct((112, 128), F32),
+            jax.ShapeDtypeStruct((224, 1024), BF16),
+        ),
+        in_specs=[pl.BlockSpec(memory_space=pltpu.VMEM)] * 5,
+        out_specs=[pl.BlockSpec(memory_space=pltpu.HBM)] * 3,
+        scratch_shapes=[
+            vmem((112, 128), F32),
+            vmem((112, 128), F32),
+            vmem((224, 1024), BF16),
+            pltpu.SemaphoreType.DMA((4,)),
+        ],
+        compiler_params=pltpu.CompilerParams(vmem_limit_bytes=16 << 20),
+        name="finish_step",
+    )(low_rank_grad, directions, projection_basis, first, second)
     return (
         new_first.reshape(first_moment.shape),
         new_second.reshape(second_moment.shape),

time: 62.9 us -> 62.2 us (0.989)
  matrix products: 1.26 us -> 0 us
  Pallas kernels: 58.5 us -> 59.7 us
  other arithmetic: 0.66 us -> 0 us
    dot_general x1 -> x0, matrix products: 1.26 us -> none  [per_device(): lax.dot_general(directions, projection_basis, (((1,), (1,)), ((), ())), p...]
    pallas_call x0 -> x1, Pallas kernels: none -> 1.22 us  [per_device(): pl.pallas_call(finish, out_shape=(jax.ShapeDtypeStruct((112, 128), F32),...]
    add x1 -> x0, other arithmetic: 0.66 us -> none  [per_device(): new_second = 0.999 * second + 0.001 * low_rank_grad * low_rank_grad]
where the time goes in v3:
time: 62.2 us; the launch traced here: 62 us
  Pallas kernels  59.7 us (96%)
  local copies, waits for them, and re-layouts  1.63 us (3%)
  between operations  0.66 us (1%)
    pallas_call x1, Pallas kernels, per_device(): pl.pallas_call(kernel, out_shape=(jax.ShapeDtypeStruct((112, 128), F32),...  58.5 us
    unnamed x6, local copies, waits for them, and re-layouts  1.63 us

profile of v3, /device:TPU:1, one launch (start us, length us, event | category | flops | bytes accessed | tf_op | source)
XLA Modules:
  0.0 62.0 jit_solution(4082937119829454234)
XLA Ops:
  0.6 0.0 copy-start.1
  0.6 0.8 %copy-done.1 = f32[1,1,28,512]{3,1,2,0:T(1,128)S(1)} copy-done((f32[1,1,28,512]{3,1,2,0:T(1,128)S(1)}, f32[1,1,28,512]{3,1,2,0:T(1,128)}, u32[]{:S(2)}) %copy-start.1) | copy-done | bytes 57368
  1.5 0.0 copy-start.2
  1.5 0.8 %copy-done.2 = f32[1,1,28,512]{3,1,2,0:T(1,128)S(1)} copy-done((f32[1,1,28,512]{3,1,2,0:T(1,128)S(1)}, f32[1,1,28,512]{3,1,2,0:T(1,128)}, u32[]{:S(2)}) %copy-start.2) | copy-done | bytes 57368
  2.3 0.0 copy-start
  2.3 58.5 %galore_step.1 = (f32[112,128]{1,0:T(8,128)S(1)}, bf16[224,512]{1,0:T(8,128)(2,1)S(1)}) custom-call(bf16[512,1024]{1,0:T(8,128)(2,1)} %act_hbm.1, bf16[1024,512]{1,0:T(8,128)(2,1)} %basis_ref.1, bf16[1792,512]{1,0:T(8,128)(2,1)} %bitcast.14, f32[112,128]{1,0:T(8,128)S(1)} %bitcast.10, f32[112,128]{1,0:T(8,128)S(1)} %bitcast.12), custom_call_target="tpu_custom_call" | custom-call | tf_op jit(solution)/shard_map/galore_step/pallas_call | solution.py:365
  60.7 0.0 copy-done
  60.8 1.2 %finish_step.1 = (f32[112,128]{1,0:T(8,128)}, f32[112,128]{1,0:T(8,128)}, bf16[224,1024]{1,0:T(8,128)(2,1)}) custom-call(f32[112,128]{1,0:T(8,128)S(1)} %get-tuple-element.8.grad_ref, bf16[224,512]{1,0:T(8,128)(2,1)S(1)} %get-tuple-element.9.lhs_ref, bf16[1024,512]{1,0:T(8,128)(2,1)S(1)} %copy-done, f32[112,128]{1,0:T(8,128)S(1)} %bitcast.11, ...), custom_call_target="tpu_custom_call" | custom-call | tf_op jit(solution)/shard_map/finish_step/pallas_call | solution.py:410
Async XLA Ops:
  0.6 0.8 %copy-start.1 = (f32[1,1,28,512]{3,1,2,0:T(1,128)S(1)}, f32[1,1,28,512]{3,1,2,0:T(1,128)}, u32[]{:S(2)}) copy-start(f32[1,1,28,512]{3,1,2,0:T(1,128)} %param.8) | copy-start | bytes 172036
  1.5 0.8 %copy-start.2 = (f32[1,1,28,512]{3,1,2,0:T(1,128)S(1)}, f32[1,1,28,512]{3,1,2,0:T(1,128)}, u32[]{:S(2)}) copy-start(f32[1,1,28,512]{3,1,2,0:T(1,128)} %param.9) | copy-start | bytes 172036
  2.3 58.5 %copy-start = (bf16[1024,512]{1,0:T(8,128)(2,1)S(1)}, bf16[1024,512]{1,0:T(8,128)(2,1)}, u32[]{:S(2)}) copy-start(bf16[1024,512]{1,0:T(8,128)(2,1)} %basis_ref.1) | copy-start | bytes 3145732
